TPU v7x, 32 devices: a whole 2x2x4 slice. The times are simulated.
32 devices in a mesh: cand: 8 (over y, x, core), rel: 4 (over z).
Axes of the slice: x: 2, y: 2, z: 4, core: 2. Of those that a mesh axis runs over, the one named last changes fastest.
Arguments:
- source_rows: bfloat16 [65536, 512], P(('cand', 'rel')), may hold values from -6 to 6
- rel_ids: int32 [65536, 1], P(('cand', 'rel')), may hold values from 0 to 7; in each aligned block of 2048 rows (0 to 2047, 2048 to 4095, ...) at most 512 rows name the same one
- relations: bfloat16 [8, 512, 512], P('rel'), may hold values from -0.25 to 0.25
- entities: float32 [8192, 512], P(('cand', 'rel')), may hold values from -0.3 to 0.3
- pos_slot: int32 [65536], P(('cand', 'rel')), may hold values from 0 to 2047
- negatives: int32 [8, 65536, 16], P(None, ('cand', 'rel')), may hold values from 0 to 255
Outputs:
- updated_entities: float32 [8192, 512], P(('cand', 'rel'))
- source_grad: bfloat16 [65536, 512], P(('cand', 'rel'))
- relation_grad: float32 [512, 8, 512], P('cand', 'rel')
Inputs may be any that keep to these rules, and one draw needn't show every extreme that they name: `rel_ids`: in each aligned block of 2048 rows (the rows of one device) no relation is named by more than 512 rows, a bound that some block reaches.
All inputs are finite; a program needn't handle non-finite values.
Results may differ from a plain program's by a relative error of at most 0.019.
Values may be sent and summed in bfloat16 or wider, within the bound.
No kernel may reach another device: no remote copies, remote signals or barrier semaphores. Data moves between devices by JAX's collectives and lax.ppermute only.
A program may use at most 128 MiB of HBM per device.

v0:
```python
import jax
import jax.numpy as jnp
from jax import lax
from jax.sharding import PartitionSpec as P

STOPS = 8


learn_rate = 0.005


def from_behind(block, axis, distance):
    devices = range(lax.axis_size(axis))
    route = [((i - distance) % len(devices), i) for i in devices]
    return lax.ppermute(block, axis, route)


def slot_index(rel_ids, nrel, most):
    ids = rel_ids[:, 0]
    onehot = (ids[:, None] == jnp.arange(nrel, dtype=jnp.int32)[None, :]).astype(jnp.int32)
    rank = jnp.cumsum(onehot, axis=0) - onehot
    return ids * most + jnp.sum(rank * onehot, axis=1)


def place_rows(rows, slot, total):
    return jnp.zeros((total, rows.shape[1]), rows.dtype).at[slot].set(rows)


def shards(source_rows, rel_ids, relations, entities, pos_slot, negatives):
    src_rows, width = source_rows.shape
    rel_dev = relations.shape[0]
    owners = lax.axis_size("rel")
    nrel = rel_dev * owners
    most = 2 * src_rows // nrel
    slot = slot_index(rel_ids, nrel, most)
    sent = place_rows(source_rows, slot, nrel * most).reshape(nrel, most, width)
    every_matrix = lax.all_gather(relations, "rel", axis=0, tiled=True)
    q_slots = jnp.einsum(
        "kmd,kde->kme", sent, every_matrix, preferred_element_type=jnp.float32
    ).astype(jnp.bfloat16)
    queries = q_slots.reshape(nrel * most, width)[slot]
    part_rows = entities.shape[0]
    columns = jnp.arange(part_rows, dtype=jnp.int32)
    state = entities
    query_acc = jnp.zeros((src_rows, width), jnp.float32)
    for stop in range(STOPS):
        if stop > 0:
            state = from_behind(state, "cand", 1)
        wide = state.astype(jnp.bfloat16)
        logits = lax.dot_general(
            queries, wide, (((1,), (1,)), ((), ())), preferred_element_type=jnp.float32
        )
        picks = negatives[stop]
        counts = jnp.zeros(logits.shape, jnp.float32)
        for sample in range(picks.shape[1]):
            counts = counts + (picks[:, sample][:, None] == columns[None, :]).astype(jnp.float32)
        hits = (pos_slot[:, None] == stop * part_rows + columns[None, :]).astype(jnp.float32)
        weight = (counts * jax.nn.sigmoid(logits) - hits * jax.nn.sigmoid(-logits)).astype(
            jnp.bfloat16
        )
        query_acc = query_acc + jnp.dot(weight, wide, preferred_element_type=jnp.float32)
        change = lax.dot_general(
            weight, queries, (((0,), (0,)), ((), ())), preferred_element_type=jnp.float32
        )
        state = state - learn_rate * change
    query_grad = query_acc.astype(jnp.bfloat16)
    gq_slots = place_rows(query_grad, slot, nrel * most).reshape(nrel, most, width)
    back_slots = jnp.einsum(
        "kme,kde->kmd", gq_slots, every_matrix, preferred_element_type=jnp.float32
    ).astype(jnp.bfloat16)
    terms = jnp.einsum("kmd,kme->dke", sent, gq_slots, preferred_element_type=jnp.float32)
    partial_value = lax.psum_scatter(
        terms.astype(jnp.bfloat16), "rel", scatter_dimension=1, tiled=True
    )
    source_grad = back_slots.reshape(nrel * most, width)[slot]
    relation_grad = lax.psum_scatter(partial_value, "cand", scatter_dimension=0, tiled=True).astype(
        jnp.float32
    )
    return (state, source_grad, relation_grad)


def solution(mesh):
    placed = (
        P(("cand", "rel"), None),
        P(("cand", "rel"), None),
        P("rel", None, None),
        P(("cand", "rel"), None),
        P(("cand", "rel")),
        P(None, ("cand", "rel"), None),
    )
    return jax.shard_map(
        shards,
        mesh=mesh,
        in_specs=placed,
        out_specs=(P(("cand", "rel"), None), P(("cand", "rel"), None), P("cand", "rel", None)),
        check_vma=False,
    )
```

profile of v0, /device:TPU:0, one launch (start us, length us, event | category | flops | bytes accessed | tf_op | source)
XLA Modules:
  0.0 399.5 jit_solution(10047279410377836420)
XLA Ops:
  13.0 12.7 %scatter_custom_fusion = bf16[4096,512]{1,0:T(8,128)(2,1)} fusion(s32[2048]{0:T(1024)S(1)} %bitcast.221, bf16[2048,512]{1,0:T(8,128)(2,1)} %param.6, bf16[]{:T(256)} %constant.14.clone.1), kind=kCustom, calls=%fused_computation.131 | custom fusion | bytes 4194816 | tf_op jit(solution)/shard_map/scatter | solution.py:26
  30.0 63.1 %all-gather.2.cloned.1.call-done = bf16[8,512,512]{2,1,0:T(8,128)(2,1)} async-done(((bf16[2,512,512]{2,1,0:T(8,128)(2,1)}), bf16[8,512,512]{2,1,0:T(8,128)(2,1)}) %all-gather.2.cloned.1.call-update) | async-done | bytes 4194320 | tf_op jit(solution)/shard_map/all_gather | solution.py:37
  93.1 7.9 %convolution_convert_fusion.1 = bf16[8,512,512]{2,1,0:T(8,128)(2,1)} fusion(bf16[8,512,512]{2,1,0:T(8,128)(2,1)} %bitcast.216, bf16[8,512,512]{2,1,0:T(8,128)(2,1)} %all-gather.2.cloned.1.call-done), kind=kOutput, calls=%fused_computation.7 | convolution fusion | flops 2149580800 | bytes 12582912 | tf_op jit(solution)/shard_map/kmd,kde->kme/dot_general | solution.py:38
  101.0 10.4 %gather_fusion = bf16[2048,512]{1,0:T(8,128)(2,1)S(1)} fusion(bf16[4096,512]{1,0:T(8,128)(2,1)} %bitcast.213, s32[2048]{0:T(1024)S(1)} %broadcast_clamp_fusion), kind=kCustom, calls=%fused_computation | custom fusion | bytes 4202496 | tf_op jit(solution)/shard_map/gather | solution.py:41
  111.4 5.2 %subtract_convert_fusion.7 = bf16[2048,256]{1,0:T(8,128)(2,1)S(1)} fusion(s32[2048]{0:T(1024)S(1)} %bitcast.338, s32[2048]{0:T(1024)S(1)} %bitcast.339, s32[2048]{0:T(1024)S(1)} %bitcast.340, s32[2048]{0:T(1024)S(1)} %bitcast.341, s32[2048]{0:T(1024)S(1)} %bitcast.342, s32[2048]{0:T(1024)S(1)} %bitcast.343, s32[2048]{0:T(1024)S(1)} %bitcast.344, ...), kind=kOutput, calls=%fused_computation.128 | convolution fusion | flops 566886400 | bytes 3809280 | tf_op jit(solution)/shard_map/dot_general | solution.py:50
  117.9 9.4 %collective-permute-done = f32[256,512]{1,0:T(8,128)S(1)} collective-permute-done((f32[256,512]{1,0:T(8,128)S(1)}, f32[256,512]{1,0:T(8,128)S(1)}, u32[]{:S(2)}, u32[]{:S(2)}) %collective-permute-start) | collective-permute-done | bytes 524320 | tf_op jit(solution)/shard_map/ppermute | solution.py:15
  127.4 5.2 %subtract_convert_fusion.6 = bf16[2048,256]{1,0:T(8,128)(2,1)S(1)} fusion(s32[256]{0:T(256)S(1)} %copy-done.73, s32[2048]{0:T(1024)S(1)} %bitcast.322, s32[2048]{0:T(1024)S(1)} %bitcast.323, s32[2048]{0:T(1024)S(1)} %bitcast.324, s32[2048]{0:T(1024)S(1)} %bitcast.325, s32[2048]{0:T(1024)S(1)} %bitcast.326, s32[2048]{0:T(1024)S(1)} %bitcast.327, ...), kind=kOutput, calls=%fused_computation.111 | convolution fusion | flops 566886400 | bytes 3810304 | tf_op jit(solution)/shard_map/dot_general | solution.py:50
  133.7 9.4 %collective-permute-done.1 = f32[256,512]{1,0:T(8,128)S(1)} collective-permute-done((f32[256,512]{1,0:T(8,128)S(1)}, f32[256,512]{1,0:T(8,128)S(1)}, u32[]{:S(2)}, u32[]{:S(2)}) %collective-permute-start.1) | collective-permute-done | bytes 524320 | tf_op jit(solution)/shard_map/ppermute | solution.py:15
  143.2 5.2 %subtract_convert_fusion.5 = bf16[2048,256]{1,0:T(8,128)(2,1)S(1)} fusion(s32[256]{0:T(256)S(1)} %copy-done.72, s32[2048]{0:T(1024)S(1)} %bitcast.306, s32[2048]{0:T(1024)S(1)} %bitcast.307, s32[2048]{0:T(1024)S(1)} %bitcast.308, s32[2048]{0:T(1024)S(1)} %bitcast.309, s32[2048]{0:T(1024)S(1)} %bitcast.310, s32[2048]{0:T(1024)S(1)} %bitcast.311, ...), kind=kOutput, calls=%fused_computation.94 | convolution fusion | flops 566886400 | bytes 3810304 | tf_op jit(solution)/shard_map/dot_general | solution.py:50
  149.5 9.4 %collective-permute-done.2 = f32[256,512]{1,0:T(8,128)S(1)} collective-permute-done((f32[256,512]{1,0:T(8,128)S(1)}, f32[256,512]{1,0:T(8,128)S(1)}, u32[]{:S(2)}, u32[]{:S(2)}) %collective-permute-start.2) | collective-permute-done | bytes 524320 | tf_op jit(solution)/shard_map/ppermute | solution.py:15
  159.0 5.2 %subtract_convert_fusion.4 = bf16[2048,256]{1,0:T(8,128)(2,1)S(1)} fusion(s32[256]{0:T(256)S(1)} %iota_add_fusion.4, s32[2048]{0:T(1024)S(1)} %bitcast.242, s32[2048]{0:T(1024)S(1)} %bitcast.243, s32[2048]{0:T(1024)S(1)} %bitcast.244, s32[2048]{0:T(1024)S(1)} %bitcast.245, s32[2048]{0:T(1024)S(1)} %bitcast.246, s32[2048]{0:T(1024)S(1)} %bitcast.247, ...), kind=kOutput, calls=%fused_computation.77 | convolution fusion | flops 566886400 | bytes 3810304 | tf_op jit(solution)/shard_map/dot_general | solution.py:50
  165.2 2.8 fusion.54
  168.0 6.5 %collective-permute-done.3 = f32[256,512]{1,0:T(8,128)S(1)} collective-permute-done((f32[256,512]{1,0:T(8,128)S(1)}, f32[256,512]{1,0:T(8,128)S(1)}, u32[]{:S(2)}, u32[]{:S(2)}) %collective-permute-start.3) | collective-permute-done | bytes 524320 | tf_op jit(solution)/shard_map/ppermute | solution.py:15
  174.6 5.2 %subtract_convert_fusion.3 = bf16[2048,256]{1,0:T(8,128)(2,1)S(1)} fusion(s32[256]{0:T(256)S(1)} %iota_add_fusion.3, s32[2048]{0:T(1024)S(1)} %bitcast.226, s32[2048]{0:T(1024)S(1)} %bitcast.227, s32[2048]{0:T(1024)S(1)} %bitcast.228, s32[2048]{0:T(1024)S(1)} %bitcast.229, s32[2048]{0:T(1024)S(1)} %bitcast.230, s32[2048]{0:T(1024)S(1)} %bitcast.231, ...), kind=kOutput, calls=%fused_computation.60 | convolution fusion | flops 566886400 | bytes 3810304 | tf_op jit(solution)/shard_map/dot_general | solution.py:50
  180.8 2.8 fusion.48
  186.3 4.0 %collective-permute-done.4 = f32[256,512]{1,0:T(8,128)S(1)} collective-permute-done((f32[256,512]{1,0:T(8,128)S(1)}, f32[256,512]{1,0:T(8,128)S(1)}, u32[]{:S(2)}, u32[]{:S(2)}) %collective-permute-start.4) | collective-permute-done | bytes 524320 | tf_op jit(solution)/shard_map/ppermute | solution.py:15
  190.3 5.2 %subtract_convert_fusion.2 = bf16[2048,256]{1,0:T(8,128)(2,1)S(1)} fusion(s32[256]{0:T(256)S(1)} %iota_add_fusion.2, s32[2048]{0:T(1024)S(1)} %bitcast.258, s32[2048]{0:T(1024)S(1)} %bitcast.259, s32[2048]{0:T(1024)S(1)} %bitcast.260, s32[2048]{0:T(1024)S(1)} %bitcast.261, s32[2048]{0:T(1024)S(1)} %bitcast.262, s32[2048]{0:T(1024)S(1)} %bitcast.263, ...), kind=kOutput, calls=%fused_computation.43 | convolution fusion | flops 566886400 | bytes 3810304 | tf_op jit(solution)/shard_map/dot_general | solution.py:50
  196.3 2.8 fusion.36
  201.7 4.1 %collective-permute-done.5 = f32[256,512]{1,0:T(8,128)S(1)} collective-permute-done((f32[256,512]{1,0:T(8,128)S(1)}, f32[256,512]{1,0:T(8,128)S(1)}, u32[]{:S(2)}, u32[]{:S(2)}) %collective-permute-start.5) | collective-permute-done | bytes 524320 | tf_op jit(solution)/shard_map/ppermute | solution.py:15
  205.8 5.1 %subtract_convert_fusion.1 = bf16[2048,256]{1,0:T(8,128)(2,1)S(1)} fusion(s32[256]{0:T(256)S(1)} %iota_add_fusion.1, s32[2048]{0:T(1024)S(1)} %bitcast.274, s32[2048]{0:T(1024)S(1)} %bitcast.275, s32[2048]{0:T(1024)S(1)} %bitcast.276, s32[2048]{0:T(1024)S(1)} %bitcast.277, s32[2048]{0:T(1024)S(1)} %bitcast.278, s32[2048]{0:T(1024)S(1)} %bitcast.279, ...), kind=kOutput, calls=%fused_computation.26 | convolution fusion | flops 566886400 | bytes 3810304 | tf_op jit(solution)/shard_map/dot_general | solution.py:50
  212.0 2.8 fusion.24
  214.8 2.7 fusion.18
  217.5 3.9 collective-permute-done.6
  221.5 5.2 %subtract_convert_fusion = bf16[2048,256]{1,0:T(8,128)(2,1)S(1)} fusion(s32[256]{0:T(256)S(1)} %iota_add_fusion, s32[2048]{0:T(1024)S(1)} %bitcast.290, s32[2048]{0:T(1024)S(1)} %bitcast.291, s32[2048]{0:T(1024)S(1)} %bitcast.292, s32[2048]{0:T(1024)S(1)} %bitcast.293, s32[2048]{0:T(1024)S(1)} %bitcast.294, s32[2048]{0:T(1024)S(1)} %bitcast.295, ...), kind=kOutput, calls=%fused_computation.9 | convolution fusion | flops 566886400 | bytes 3810304 | tf_op jit(solution)/shard_map/dot_general | solution.py:50
  226.7 2.7 fusion.12
  229.4 17.8 %scatter_custom_fusion.1 = bf16[4096,512]{1,0:T(8,128)(2,1)} fusion(s32[2048]{0:T(1024)} %bitcast.223, f32[2048,512]{1,0:T(8,128)} %fusion.12, f32[2048,512]{1,0:T(8,128)} %fusion.18, f32[2048,512]{1,0:T(8,128)} %fusion.24, f32[2048,512]{1,0:T(8,128)} %fusion.30, f32[2048,512]{1,0:T(8,128)} %fusion.36, f32[2048,512]{1,0:T(8,128)} %fusion.42, ...), kind=kCustom, calls=%fused_computation.8 | custom fusion | flops 8388608 | bytes 37749248 | tf_op jit(solution)/shard_map/scatter | solution.py:26
  247.2 7.9 %convert_bitcast_fusion = bf16[512,8,512]{0,2,1:T(8,128)(2,1)} fusion(bf16[8,512,512]{2,1,0:T(8,128)(2,1)} %bitcast.214, bf16[8,512,512]{2,1,0:T(8,128)(2,1)} %bitcast.217), kind=kOutput, calls=%fused_computation.4 | convolution fusion | flops 2149580800 | bytes 12582912 | tf_op jit(solution)/shard_map/kmd,kme->dke/dot_general | solution.py:71
  257.0 72.7 %reduce-scatter.2.cloned.1.call-done = bf16[512,2,512]{0,2,1:T(8,128)(2,1)} async-done(((bf16[512,8,512]{0,2,1:T(8,128)(2,1)}), bf16[512,2,512]{0,2,1:T(8,128)(2,1)}) %reduce-scatter.2.cloned.1.call-update) | async-done | bytes 1048592 | tf_op jit(solution)/shard_map/reduce_scatter | solution.py:72
  329.7 3.7 copy.14
  333.4 7.9 %convolution_convert_fusion = bf16[8,512,512]{2,1,0:T(8,128)(2,1)} fusion(bf16[8,512,512]{2,1,0:T(8,128)(2,1)} %bitcast.215, bf16[8,512,512]{2,1,0:T(8,128)(2,1)} %all-gather.2.cloned.1.call-done), kind=kOutput, calls=%fused_computation.6 | convolution fusion | flops 2149580800 | bytes 12582912 | tf_op jit(solution)/shard_map/kme,kde->kmd/dot_general | solution.py:68
  341.3 12.0 %gather_fusion.1 = bf16[2048,512]{1,0:T(8,128)(2,1)} fusion(bf16[4096,512]{1,0:T(8,128)(2,1)} %bitcast.212, s32[2048]{0:T(1024)S(1)} %copy-done.4), kind=kCustom, calls=%fused_computation.1 | custom fusion | bytes 4202496 | tf_op jit(solution)/shard_map/gather | solution.py:75
  355.9 34.9 %all-reduce.3.cloned.1.call-done = bf16[512,2,512]{2,1,0:T(2,128)(2,1)} async-done(((bf16[512,2,512]{2,1,0:T(2,128)(2,1)}), bf16[512,2,512]{2,1,0:T(2,128)(2,1)}) %all-reduce.3.cloned.1.call-update) | async-done | bytes 1048592
  (197 shorter events, 27.6 us)
Async XLA Ops:
  7.2 85.9 %all-gather.2.cloned.1.call-start = ((), (), s32[]{:S(2)}) async-start(), calls=%async_computation.1 | async-start | bytes 5242880 | tf_op jit(solution)/shard_map/all_gather | solution.py:37
  7.9 321.8 %reduce-scatter.2.cloned.1.call-start = ((), (), s32[]{:S(2)}) async-start(), calls=%async_computation.2 | async-start | bytes 5242880 | tf_op jit(solution)/shard_map/reduce_scatter | solution.py:72
  12.9 13.9 %copy-start.5 = (s32[2048,1]{0,1:T(1,128)}, s32[2048,1]{0,1:T(1,128)S(1)}, u32[]{:S(2)}) copy-start(s32[2048,1]{0,1:T(1,128)S(1)} %compare_select_fusion) | copy-start | bytes 24580
  12.9 13.8 %copy-start = (s32[8,2048,16]{1,2,0:T(8,128)S(1)}, s32[8,2048,16]{1,2,0:T(8,128)}, u32[]{:S(2)}) copy-start(s32[8,2048,16]{1,2,0:T(8,128)} %param.11) | copy-start | bytes 3145732
  26.8 74.2 %copy-start.3 = (s32[2048]{0:T(1024)}, s32[2048]{0:T(1024)S(1)}, u32[]{:S(2)}) copy-start(s32[2048]{0:T(1024)S(1)} %broadcast_clamp_fusion) | copy-start | bytes 24580
  116.6 10.7 %copy-start.53 = (s32[2048,1]{0,1:T(1,128)S(1)}, s32[2048,1]{0,1:T(1,128)}, u32[]{:S(2)}) copy-start(s32[2048,1]{0,1:T(1,128)} %get-tuple-element.113) | copy-start | bytes 24580
  116.6 10.6 %copy-start.54 = (s32[2048,1]{0,1:T(1,128)S(1)}, s32[2048,1]{0,1:T(1,128)}, u32[]{:S(2)}) copy-start(s32[2048,1]{0,1:T(1,128)} %get-tuple-element.114) | copy-start | bytes 24580
  116.6 10.6 %copy-start.55 = (s32[2048,1]{0,1:T(1,128)S(1)}, s32[2048,1]{0,1:T(1,128)}, u32[]{:S(2)}) copy-start(s32[2048,1]{0,1:T(1,128)} %get-tuple-element.115) | copy-start | bytes 24580
  116.6 10.6 %copy-start.56 = (s32[2048,1]{0,1:T(1,128)S(1)}, s32[2048,1]{0,1:T(1,128)}, u32[]{:S(2)}) copy-start(s32[2048,1]{0,1:T(1,128)} %get-tuple-element.116) | copy-start | bytes 24580
  116.6 10.6 %copy-start.57 = (s32[2048,1]{0,1:T(1,128)S(1)}, s32[2048,1]{0,1:T(1,128)}, u32[]{:S(2)}) copy-start(s32[2048,1]{0,1:T(1,128)} %get-tuple-element.117) | copy-start | bytes 24580
  116.7 10.6 %copy-start.58 = (s32[2048,1]{0,1:T(1,128)S(1)}, s32[2048,1]{0,1:T(1,128)}, u32[]{:S(2)}) copy-start(s32[2048,1]{0,1:T(1,128)} %get-tuple-element.118) | copy-start | bytes 24580
  116.7 10.6 %copy-start.59 = (s32[2048,1]{0,1:T(1,128)S(1)}, s32[2048,1]{0,1:T(1,128)}, u32[]{:S(2)}) copy-start(s32[2048,1]{0,1:T(1,128)} %get-tuple-element.119) | copy-start | bytes 24580
  116.7 10.6 %copy-start.60 = (s32[2048,1]{0,1:T(1,128)S(1)}, s32[2048,1]{0,1:T(1,128)}, u32[]{:S(2)}) copy-start(s32[2048,1]{0,1:T(1,128)} %get-tuple-element.120) | copy-start | bytes 24580
  116.7 10.6 %copy-start.61 = (s32[2048,1]{0,1:T(1,128)S(1)}, s32[2048,1]{0,1:T(1,128)}, u32[]{:S(2)}) copy-start(s32[2048,1]{0,1:T(1,128)} %get-tuple-element.121) | copy-start | bytes 24580
  116.7 10.6 %copy-start.62 = (s32[2048,1]{0,1:T(1,128)S(1)}, s32[2048,1]{0,1:T(1,128)}, u32[]{:S(2)}) copy-start(s32[2048,1]{0,1:T(1,128)} %get-tuple-element.122) | copy-start | bytes 24580
  116.7 10.6 %copy-start.63 = (s32[2048,1]{0,1:T(1,128)S(1)}, s32[2048,1]{0,1:T(1,128)}, u32[]{:S(2)}) copy-start(s32[2048,1]{0,1:T(1,128)} %get-tuple-element.123) | copy-start | bytes 24580
  116.7 10.6 %copy-start.64 = (s32[2048,1]{0,1:T(1,128)S(1)}, s32[2048,1]{0,1:T(1,128)}, u32[]{:S(2)}) copy-start(s32[2048,1]{0,1:T(1,128)} %get-tuple-element.124) | copy-start | bytes 24580
  116.7 10.6 %copy-start.65 = (s32[2048,1]{0,1:T(1,128)S(1)}, s32[2048,1]{0,1:T(1,128)}, u32[]{:S(2)}) copy-start(s32[2048,1]{0,1:T(1,128)} %get-tuple-element.125) | copy-start | bytes 24580
  116.7 10.6 %copy-start.66 = (s32[2048,1]{0,1:T(1,128)S(1)}, s32[2048,1]{0,1:T(1,128)}, u32[]{:S(2)}) copy-start(s32[2048,1]{0,1:T(1,128)} %get-tuple-element.126) | copy-start | bytes 24580
  116.7 10.6 %copy-start.67 = (s32[2048,1]{0,1:T(1,128)S(1)}, s32[2048,1]{0,1:T(1,128)}, u32[]{:S(2)}) copy-start(s32[2048,1]{0,1:T(1,128)} %get-tuple-element.127) | copy-start | bytes 24580
  116.8 10.6 %copy-start.68 = (s32[2048,1]{0,1:T(1,128)S(1)}, s32[2048,1]{0,1:T(1,128)}, u32[]{:S(2)}) copy-start(s32[2048,1]{0,1:T(1,128)} %get-tuple-element.128) | copy-start | bytes 24580
  116.8 10.6 %copy-start.70 = (s32[2048]{0:T(1024)S(1)}, s32[2048]{0:T(1024)}, u32[]{:S(2)}) copy-start(s32[2048]{0:T(1024)} %param.10) | copy-start | bytes 24580
  116.8 10.6 %copy-start.73 = (s32[256]{0:T(256)S(1)}, s32[256]{0:T(256)}, u32[]{:S(2)}) copy-start(s32[256]{0:T(256)} %iota_add_fusion.6) | copy-start | bytes 3076
  117.5 9.7 %collective-permute-start = (f32[256,512]{1,0:T(8,128)S(1)}, f32[256,512]{1,0:T(8,128)S(1)}, u32[]{:S(2)}, u32[]{:S(2)}) collective-permute-start(f32[256,512]{1,0:T(8,128)S(1)} %fusion.11), channel_id=1, source_target_pairs={{28,0},{0,4},{4,8},{8,12},{12,16},{16,20},{20,24},{24,28},{29,1},{... | collective-permute-start | bytes 1572872 | tf_op jit(solution)/shard_map/ppermute | solution.py:15
  132.6 10.5 %copy-start.37 = (s32[2048,1]{0,1:T(1,128)S(1)}, s32[2048,1]{0,1:T(1,128)}, u32[]{:S(2)}) copy-start(s32[2048,1]{0,1:T(1,128)} %get-tuple-element.97) | copy-start | bytes 24580
  133.5 9.6 %collective-permute-start.1 = (f32[256,512]{1,0:T(8,128)S(1)}, f32[256,512]{1,0:T(8,128)S(1)}, u32[]{:S(2)}, u32[]{:S(2)}) collective-permute-start(f32[256,512]{1,0:T(8,128)S(1)} %fusion.10), channel_id=1, source_target_pairs={{28,0},{0,4},{4,8},{8,12},{12,16},{16,20},{20,24},{24,28},{29,1},{... | collective-permute-start | bytes 1572872 | tf_op jit(solution)/shard_map/ppermute | solution.py:15
  149.3 9.6 %collective-permute-start.2 = (f32[256,512]{1,0:T(8,128)S(1)}, f32[256,512]{1,0:T(8,128)S(1)}, u32[]{:S(2)}, u32[]{:S(2)}) collective-permute-start(f32[256,512]{1,0:T(8,128)S(1)} %fusion.9), channel_id=1, source_target_pairs={{28,0},{0,4},{4,8},{8,12},{12,16},{16,20},{20,24},{24,28},{29,1},{... | collective-permute-start | bytes 1572872 | tf_op jit(solution)/shard_map/ppermute | solution.py:15
  164.9 9.6 %collective-permute-start.3 = (f32[256,512]{1,0:T(8,128)S(1)}, f32[256,512]{1,0:T(8,128)S(1)}, u32[]{:S(2)}, u32[]{:S(2)}) collective-permute-start(f32[256,512]{1,0:T(8,128)S(1)} %fusion.8), channel_id=1, source_target_pairs={{28,0},{0,4},{4,8},{8,12},{12,16},{16,20},{20,24},{24,28},{29,1},{... | collective-permute-start | bytes 1572872 | tf_op jit(solution)/shard_map/ppermute | solution.py:15
  180.6 9.8 %collective-permute-start.4 = (f32[256,512]{1,0:T(8,128)S(1)}, f32[256,512]{1,0:T(8,128)S(1)}, u32[]{:S(2)}, u32[]{:S(2)}) collective-permute-start(f32[256,512]{1,0:T(8,128)S(1)} %fusion.7), channel_id=1, source_target_pairs={{28,0},{0,4},{4,8},{8,12},{12,16},{16,20},{20,24},{24,28},{29,1},{... | collective-permute-start | bytes 1572872 | tf_op jit(solution)/shard_map/ppermute | solution.py:15
  196.2 9.6 %collective-permute-start.5 = (f32[256,512]{1,0:T(8,128)S(1)}, f32[256,512]{1,0:T(8,128)S(1)}, u32[]{:S(2)}, u32[]{:S(2)}) collective-permute-start(f32[256,512]{1,0:T(8,128)S(1)} %fusion.6), channel_id=1, source_target_pairs={{28,0},{0,4},{4,8},{8,12},{12,16},{16,20},{20,24},{24,28},{29,1},{... | collective-permute-start | bytes 1572872 | tf_op jit(solution)/shard_map/ppermute | solution.py:15
  211.7 9.8 %collective-permute-start.6 = (f32[256,512]{1,0:T(8,128)S(1)}, f32[256,512]{1,0:T(8,128)S(1)}, u32[]{:S(2)}, u32[]{:S(2)}) collective-permute-start(f32[256,512]{1,0:T(8,128)S(1)} %fusion.5), channel_id=1, source_target_pairs={{28,0},{0,4},{4,8},{8,12},{12,16},{16,20},{20,24},{24,28},{29,1},{... | collective-permute-start | bytes 1572872 | tf_op jit(solution)/shard_map/ppermute | solution.py:15
  255.2 135.6 %all-reduce.3.cloned.1.call-start = ((), (), s32[]{:S(2)}) async-start(), calls=%async_computation.3 | async-start | bytes 2097152
  (52 other events, 510.5 us)
Sparse Core Ops, SparseCore 0:
  9.6 83.4 all-gather.1
  255.3 74.3 reduce-scatter.1
  333.5 57.1 all-reduce.2
where the time goes:
time: 407 us; the launch traced here: 399 us
  waiting for transfers between devices  218 us (54%)
  matrix products  94.7 us (23%)
  local copies, waits for them, and re-layouts  43.6 us (11%)
  other arithmetic  25.4 us (6%)
  between operations  16.2 us (4%)
    reduce_scatter x1, waiting for transfers between devices, shards(): lax.psum_scatter(terms.astype(jnp.bfloat16), 'rel', scatter_dimension=1,...  72.7 us
    all_gather x1, waiting for transfers between devices, shards(): every_matrix = lax.all_gather(relations, 'rel', axis=0, tiled=True)  63.1 us
    ppermute x7, waiting for transfers between devices, from_behind(): return lax.ppermute(block, axis, route)  46.7 us
    dot_general x8, matrix products, shards(): lax.dot_general(queries, wide, (((1,), (1,)), ((), ())), preferred_elemen...  41.4 us
    unnamed x4, waiting for transfers between devices  35.6 us
    dot_general x8, matrix products, shards(): jnp.dot(weight, wide, preferred_element_type=jnp.float32)  21.9 us
    scatter x1, other arithmetic, place_rows(): return jnp.zeros((total, rows.shape[1]), rows.dtype).at[slot].set(rows)  17.8 us
    scatter x1, local copies, waits for them, and re-layouts, place_rows(): return jnp.zeros((total, rows.shape[1]), rows.dtype).at[slot].set(rows)  12.7 us
  transfers between devices with their start and end apart: 10, of which 10 were waited for; matrix products, arithmetic and copies ran while one was open for 16% of the time, Pallas kernels for 0%

commit v1 on v0

v1 whole, which is shorter than its diff:
```python
import jax
import jax.numpy as jnp
from jax import lax
from jax.experimental import pallas as pl
from jax.experimental.pallas import tpu as pltpu
from jax.sharding import PartitionSpec as P

learn_rate = 0.005
ALIGN = 16
HALVES = 2
bf16 = jnp.bfloat16
f32 = jnp.float32
VMEM_LIMIT = 56 * 2**20


def shift(x, axis, distance):
    n = lax.axis_size(axis)
    return lax.ppermute(x, axis, [((i + distance) % n, i) for i in range(n)])


def swap(x, bit):
    return lax.ppermute(x, "cand", [(i, i ^ bit) for i in range(lax.axis_size("cand"))])


def chip_bits():
    bits, bit = [], 2
    while bit < lax.axis_size("cand"):
        bits.append(bit)
        bit *= 2
    return bits


def bit_orders():
    bits = chip_bits()
    return bits, bits[::-1]


def vmem():
    return pl.BlockSpec(memory_space=pltpu.VMEM)


def smem():
    return pl.BlockSpec(memory_space=pltpu.SMEM)


def call(kernel, out_shape, in_specs, scratch=(), flops=0, moved=0):
    return pl.pallas_call(
        kernel,
        out_shape=out_shape,
        in_specs=in_specs,
        out_specs=jax.tree.map(lambda _: vmem(), out_shape),
        scratch_shapes=scratch,
        compiler_params=pltpu.CompilerParams(vmem_limit_bytes=VMEM_LIMIT),
        cost_estimate=pl.CostEstimate(flops=flops, bytes_accessed=moved, transcendentals=0),
    )


def gather_pieces(relations):
    n, m = lax.axis_size("cand"), lax.axis_size("rel")
    width = relations.shape[-1]
    flat = relations.reshape(-1, width)
    piece = flat.shape[0] // n
    own = lax.dynamic_slice(flat, (lax.axis_index("cand") * piece, 0), (piece, width))
    came = jnp.stack([shift(own, "rel", j) for j in range(1, m)])
    half = piece // 2
    pieces = []
    for h, order in enumerate(bit_orders()):
        held = came[None, :, h * half : (h + 1) * half]
        for bit in order:
            held = jnp.concatenate([held, swap(held, bit)], 0)
        pieces.append(jnp.concatenate([held, swap(held, 1)], 0))
    return pieces


def piece_slots():
    n = lax.axis_size("cand")
    apart = jnp.arange(n, dtype=jnp.int32) ^ lax.axis_index("cand")
    tables = []
    for order in bit_orders():
        slot = jnp.zeros_like(apart)
        for place, bit in enumerate(order + [1]):
            slot = slot + jnp.where((apart & bit) != 0, 1 << place, 0)
        tables.append(slot)
    return jnp.stack(tables).astype(jnp.int32)


def load_matrix(k, me_rel, slots, relations, pieces, matrix, m):
    rel_dev, width = relations.shape[0], relations.shape[1]
    owner, which = k // rel_dev, k % rel_dev
    half = pieces[0].shape[2]
    per = width // (2 * half)
    away = lax.rem(owner - me_rel + m, m)

    @pl.when(away == 0)
    def _():
        matrix[...] = relations[which]

    @pl.when(away != 0)
    def _():
        for i in range(per):
            c = which * per + i
            for h in range(2):
                at = (2 * i + h) * half
                matrix[at : at + half, :] = pieces[h][slots[h, c], away - 1]


def group_rows(k, starts, counts, rows, most):
    first = starts[k]
    low = pl.multiple_of(jnp.minimum(first, rows - most), ALIGN)
    return low, first - low, counts[k]


def project(x, starts, counts, relations, pieces, transposed):
    m = lax.axis_size("rel")
    nrel = relations.shape[0] * m
    rows, width = x.shape
    most = 2 * (rows - nrel * ALIGN) // nrel
    me = lax.axis_index("rel").astype(jnp.int32).reshape(1)

    def kernel(me_ref, slots, starts_ref, counts_ref, x_ref, rel_ref, p0, p1, out_ref, matrix):
        out_ref[...] = jnp.zeros_like(out_ref)
        for k in range(nrel):
            load_matrix(k, me_ref[0], slots, rel_ref, (p0, p1), matrix.at[k % 2], m)
            low, skip, _ = group_rows(k, starts_ref, counts_ref, rows, most)
            dims = (((1,), (1 if transposed else 0,)), ((), ()))
            got = lax.dot_general(
                x_ref[pl.ds(low, most), :], matrix[k % 2], dims, preferred_element_type=f32
            ).astype(bf16)
            mine = lax.broadcasted_iota(jnp.int32, (most, 1), 0) >= skip
            out_ref[pl.ds(low, most), :] = jnp.where(mine, got, out_ref[pl.ds(low, most), :])

    return call(
        kernel,
        jax.ShapeDtypeStruct((rows, width), bf16),
        [smem()] * 4 + [vmem()] * 4,
        [pltpu.VMEM((2, width, width), bf16)],
        2 * nrel * most * width * width,
        0,
    )(me, piece_slots(), starts, counts, x, relations, *pieces)


def relation_terms(xs, gs, starts, counts, rel_dev, column):
    n, m = lax.axis_size("cand"), lax.axis_size("rel")
    nrel = rel_dev * m
    rows, width = xs[0].shape
    most = 2 * (rows - nrel * ALIGN) // nrel
    block, wide = width // n, width // 2
    order = bit_orders()[column]
    apart = jnp.arange(n, dtype=jnp.int32) ^ lax.axis_index("cand")
    slot = jnp.zeros_like(apart)
    for place, bit in enumerate([1] + order):
        slot = slot + jnp.where((apart & bit) != 0, n >> (place + 1), 0)
    slot = slot.astype(jnp.int32)
    away = ((lax.axis_index("rel") - jnp.arange(m)) % m).astype(jnp.int32)

    def kernel(slot_ref, away_ref, st0, ct0, st1, ct1, x0, x1, g0, g1, out_ref):
        for k in range(nrel):
            total = None
            for x_ref, g_ref, st, ct in ((x0, g0, st0, ct0), (x1, g1, st1, ct1)):
                low, skip, count = group_rows(k, st, ct, rows, most)
                row = lax.broadcasted_iota(jnp.int32, (most, 1), 0)
                mine = (row >= skip) & (row < skip + count)
                g = g_ref[pl.ds(low, most), column * wide : (column + 1) * wide]
                g = jnp.where(mine, g, jnp.zeros_like(g))
                term = lax.dot_general(
                    x_ref[pl.ds(low, most), :],
                    g,
                    (((0,), (0,)), ((), ())),
                    preferred_element_type=f32,
                )
                total = term if total is None else total + term
            total = total.astype(bf16)
            to, which = away_ref[k // rel_dev], k % rel_dev
            for b in range(n):
                out_ref[slot_ref[b], to, which] = total[b * block : (b + 1) * block]

    return call(
        kernel,
        jax.ShapeDtypeStruct((n, m, rel_dev, block, wide), bf16),
        [smem()] * 6 + [vmem()] * 4,
        (),
        4 * nrel * most * width * wide,
        0,
    )(slot, away, starts[0], counts[0], starts[1], counts[1], *xs, *gs)


def add(a, b):
    return (a.astype(f32) + b.astype(f32)).astype(bf16)


def reduce_terms(terms, column):
    n, m = lax.axis_size("cand"), lax.axis_size("rel")
    for bit in [1] + bit_orders()[column]:
        half = terms.shape[0] // 2
        terms = add(terms[:half], swap(terms[half:], bit))
    terms = terms[0]
    total = terms[0].astype(f32)
    for j in range(1, m):
        total = total + shift(terms[j], "rel", j).astype(f32)
    return total


def sort_places(rel_ids, nrel):
    ids = rel_ids[:, 0]
    rows = ids.shape[0]
    onehot = ids[None, :] == jnp.arange(nrel, dtype=jnp.int32)[:, None]
    lanes = 128
    blocks = onehot.astype(bf16).reshape(nrel, rows // lanes, lanes)
    upto = (jnp.arange(lanes)[:, None] <= jnp.arange(lanes)[None, :]).astype(bf16)
    within = lax.dot_general(
        blocks, upto, (((2,), (0,)), ((), ())), preferred_element_type=f32
    )
    sums = within[:, :, -1]
    before = jnp.cumsum(sums, axis=1) - sums
    counts = jnp.sum(sums, axis=1).astype(jnp.int32)
    padded = (counts + ALIGN - 1) // ALIGN * ALIGN
    starts = jnp.cumsum(padded) - padded
    rank = (within + before[:, :, None]).reshape(nrel, rows).astype(jnp.int32) - 1
    place = jnp.sum(jnp.where(onehot, rank + starts[:, None], 0), axis=0)
    return place, starts.astype(jnp.int32), counts


def coefficients(picks, stop, where_stop, where_row, part_rows):
    rows = picks.shape[1]
    tile = 128
    sub = 64

    def kernel(picks_ref, stop_ref, row_ref, plus_ref, minus_ref):
        for top in range(0, part_rows, sub):
            column = (lax.broadcasted_iota(jnp.int32, (sub, tile), 0) + (top + 1)).astype(f32).astype(bf16)
            one = jnp.ones((sub, tile), bf16)
            zero = jnp.zeros((sub, tile), bf16)
            for left in range(0, rows, tile):
                count = zero
                for k in range(picks_ref.shape[0]):
                    pick = picks_ref[k : k + 1, left : left + tile]
                    count = count + jnp.where(column == pick, one, zero)
                here = jnp.where(
                    stop_ref[:, left : left + tile] == float(stop + 1), row_ref[:, left : left + tile], 0.0
                ).astype(bf16)
                hit = jnp.where(column == here, one, zero)
                plus_ref[top : top + sub, left : left + tile] = (count + hit) * 0.5
                minus_ref[top : top + sub, left : left + tile] = (count - hit) * 0.5

    shape = jax.ShapeDtypeStruct((part_rows, rows), bf16)
    return call(
        kernel, (shape, shape), [vmem()] * 3, (), 2 * 10**9, 4 * part_rows * rows
    )(picks, where_stop, where_row)


def shards(source_rows, rel_ids, relations, entities, pos_slot, negatives):
    src_rows, width = source_rows.shape
    rel_dev = relations.shape[0]
    n, m = lax.axis_size("cand"), lax.axis_size("rel")
    nrel = rel_dev * m
    stops, _, samples = negatives.shape
    part_rows = entities.shape[0]
    rows = src_rows + nrel * ALIGN
    odd = lax.axis_index("cand") % 2 == 1

    pieces = gather_pieces(relations)

    place, starts, counts = sort_places(rel_ids, nrel)
    onto = (jnp.arange(rows, dtype=jnp.int32)[:, None] == place[None, :]).astype(bf16)
    x_own = jnp.dot(onto, source_rows, preferred_element_type=f32).astype(bf16)
    listed = (jnp.swapaxes(negatives, 1, 2) + 1).reshape(stops * samples, src_rows)
    wanted = jnp.stack([pos_slot // part_rows + 1, pos_slot % part_rows + 1])
    listed = jnp.concatenate([listed, wanted], 0).astype(bf16)
    listed = lax.dot_general(
        listed, onto, (((1,), (1,)), ((), ())), preferred_element_type=f32
    ).astype(bf16)
    picks = listed[: stops * samples].reshape(stops, samples, rows)
    target = listed[stops * samples :]

    x_sib = swap(x_own, 1)
    picks_sib = swap(picks[1::2], 1)
    target_sib = swap(target, 1)
    spans = swap(jnp.stack([starts, counts]), 1)
    starts_sib, counts_sib = spans[0], spans[1]

    plus, minus = [], []
    for stop in range(stops):
        chosen = picks[stop] if stop % 2 == 0 else picks_sib[stop // 2]
        aim = (target if stop % 2 == 0 else target_sib).astype(f32)
        a, b = coefficients(chosen, stop, aim[0:1], aim[1:2], part_rows)
        plus.append(a)
        minus.append(b)

    q_own = project(x_own, starts, counts, relations, pieces, False)
    q_sib = project(x_sib, starts_sib, counts_sib, relations, pieces, False)

    half = part_rows // HALVES
    state = [entities[h * half : (h + 1) * half] for h in range(HALVES)]
    acc = [None, None]
    for stop in range(stops):
        queries = q_own if stop % 2 == 0 else q_sib
        weights, wides = [], []
        for h in range(HALVES):
            cut = slice(h * half, (h + 1) * half)
            wide = state[h].astype(bf16)
            logits = lax.dot_general(
                wide, queries, (((1,), (1,)), ((), ())), preferred_element_type=f32
            )
            weight = (
                plus[stop][cut].astype(f32) * jnp.tanh(0.5 * logits) + minus[stop][cut].astype(f32)
            ).astype(bf16)
            change = jnp.dot(weight, queries, preferred_element_type=f32)
            state[h] = state[h] - learn_rate * change
            weights.append(weight)
            wides.append(wide)
            if stop + 1 < stops:
                moving = 1 - stop % 2
                route = [(i, (i + 2) % n) for i in range(n) if i % 2 == moving]
                came = lax.ppermute(state[h].astype(bf16), "cand", route)
                state[h] = jnp.where(odd == (moving == 1), came.astype(f32), state[h])
        part = lax.dot_general(
            jnp.concatenate(weights, 0),
            jnp.concatenate(wides, 0),
            (((0,), (0,)), ((), ())),
            preferred_element_type=f32,
        )
        acc[stop % 2] = part if acc[stop % 2] is None else acc[stop % 2] + part

    g_own, g_sib = acc[0].astype(bf16), acc[1].astype(bf16)
    grads = []
    for column in range(2):
        terms = relation_terms(
            (x_own, x_sib), (g_own, g_sib), (starts, starts_sib), (counts, counts_sib), rel_dev, column
        )
        grads.append(reduce_terms(terms, column))
    relation_grad = jnp.swapaxes(jnp.concatenate(grads, 2), 0, 1)

    query_grad = (acc[0] + swap(g_sib, 1).astype(f32)).astype(bf16)
    back = project(query_grad, starts, counts, relations, pieces, True)
    source_grad = lax.dot_general(
        onto, back, (((0,), (0,)), ((), ())), preferred_element_type=f32
    ).astype(bf16)
    updated = jnp.concatenate(state, 0)
    if stops % 2 == 0:
        updated = swap(updated, 1)
    return updated, source_grad, relation_grad


def solution(mesh):
    placed = (
        P(("cand", "rel"), None),
        P(("cand", "rel"), None),
        P("rel", None, None),
        P(("cand", "rel"), None),
        P(("cand", "rel")),
        P(None, ("cand", "rel"), None),
    )
    return jax.shard_map(
        shards,
        mesh=mesh,
        in_specs=placed,
        out_specs=(P(("cand", "rel"), None), P(("cand", "rel"), None), P("cand", "rel", None)),
        check_vma=False,
    )
```

time: 407 us -> 256 us (0.63)
  waiting for transfers between devices: 218 us -> 36.2 us
  Pallas kernels: 0 us -> 79.2 us
  starting transfers between devices: 1.45 us -> 60.5 us
  matrix products: 94.7 us -> 51.4 us
  local copies, waits for them, and re-layouts: 43.6 us -> 12.2 us
  other arithmetic: 25.4 us -> 10.4 us
  between operations: 16.2 us -> 2.09 us
    pallas_call x0 -> x13, Pallas kernels: none -> 79.2 us  [the longest x8 39.1 us: coefficients(): call(kernel, (shape, shape), [vmem()] * 3, (), 2 * 10 ** 9, 4 * part_rows...]
    reduce_scatter x1 -> x0, waiting for transfers between devices: 72.7 us -> none  [shards(): lax.psum_scatter(terms.astype(jnp.bfloat16), 'rel', scatter_dimension=1,...]
    all_gather x1 -> x0, waiting for transfers between devices: 63.1 us -> none  [shards(): every_matrix = lax.all_gather(relations, 'rel', axis=0, tiled=True)]
    ppermute x7 -> x41, starting transfers between devices: 1.04 us -> 60.5 us  [the longest x14 26.1 us: shards(): came = lax.ppermute(state[h].astype(bf16), 'cand', route)]
    dot_general x27 -> x44, matrix products: 94.7 us -> 51.4 us  [the longest x16 18.4 us: shards(): lax.dot_general(wide, queries, (((1,), (1,)), ((), ())), preferred_elemen...]
    unnamed x4 -> x0, waiting for transfers between devices: 35.6 us -> none
    gather x2 -> x0, local copies, waits for them, and re-layouts: 22.4 us -> none  [the longest x1 12 us: shards(): source_grad = back_slots.reshape(nrel * most, width)[slot]]
    scatter x1 -> x0, other arithmetic: 17.8 us -> none  [place_rows(): return jnp.zeros((total, rows.shape[1]), rows.dtype).at[slot].set(rows)]
  transfers between devices with their start and end apart: 10 -> 41, of which waited for: 10 -> 12; matrix products, arithmetic and copies ran while one was open for 16% -> 22% of each run, Pallas kernels for 0% -> 25%
where the time goes in v1:
time: 256 us; the launch traced here: 252 us
  Pallas kernels  79.2 us (31%)
  starting transfers between devices  60.5 us (24%)
  matrix products  51.4 us (20%)
  waiting for transfers between devices  36.2 us (14%)
  local copies, waits for them, and re-layouts  12.2 us (5%)
  other arithmetic  10.4 us (4%)
    pallas_call x8, Pallas kernels, coefficients(): call(kernel, (shape, shape), [vmem()] * 3, (), 2 * 10 ** 9, 4 * part_rows...  39.1 us
    ppermute x14, starting transfers between devices, shards(): came = lax.ppermute(state[h].astype(bf16), 'cand', route)  26.1 us
    pallas_call x3, Pallas kernels, project(): call(kernel, jax.ShapeDtypeStruct((rows, width), bf16), [smem()] * 4 + [v...  25.2 us
    ppermute x18, waiting for transfers between devices, swap(): lax.ppermute(x, 'cand', [(i, i ^ bit) for i in range(lax.axis_size('cand'...  23.8 us
    ppermute x18, starting transfers between devices, swap(): lax.ppermute(x, 'cand', [(i, i ^ bit) for i in range(lax.axis_size('cand'...  19.4 us
    dot_general x16, matrix products, shards(): lax.dot_general(wide, queries, (((1,), (1,)), ((), ())), preferred_elemen...  18.4 us
    ppermute x9, starting transfers between devices, shift(): return lax.ppermute(x, axis, [((i + distance) % n, i) for i in range(n)])  15 us
    pallas_call x2, Pallas kernels, relation_terms(): call(kernel, jax.ShapeDtypeStruct((n, m, rel_dev, block, wide), bf16), [s...  14.9 us
  transfers between devices with their start and end apart: 41, of which 12 were waited for; matrix products, arithmetic and copies ran while one was open for 22% of the time, Pallas kernels for 25%

profile of v1, /device:TPU:0, one launch (start us, length us, event | category | flops | bytes accessed | tf_op | source)
XLA Modules:
  0.0 252.0 jit_solution(1918361859443119017)
XLA Ops:
  1.7 4.1 %collective-permute-start.1 = (bf16[128,512]{1,0:T(8,128)(2,1)S(1)}, bf16[128,512]{1,0:T(8,128)(2,1)}, u32[]{:S(2)}, u32[]{:S(2)}) collective-permute-start(bf16[128,512]{1,0:T(8,128)(2,1)S(1)} %constant_dynamic-slice_fusion), channel_id=1, source_target_pairs={{2,0},{3,1},{0,2},{1,3},{6,4},{7,5},{4,6},{5,7},{10,8},{11,9},{8,1... | collective-permute-start | bytes 393224 | tf_op jit(solution)/shard_map/ppermute | solution.py:18
  11.9 6.3 %fusion.6.x_ref.x0 = bf16[2176,512]{1,0:T(8,128)(2,1)} fusion(bf16[2048,512]{1,0:T(8,128)(2,1)S(1)} %copy-done, s32[2048]{0:T(1024)S(1)} %bitcast.158), kind=kOutput, calls=%fused_computation.13 | convolution fusion | flops 4568973312 | bytes 4333568 | tf_op jit(solution)/shard_map/dot_general | solution.py:265
  20.7 3.7 %fusion.58 = bf16[130,2176]{1,0:T(8,128)(2,1)S(1)} fusion(s32[2048]{0:T(1024)S(1)} %bitcast.159, bf16[1,2048]{1,0:T(2,128)(2,1)S(1)} %stack.37, bf16[1,2048]{1,0:T(2,128)(2,1)S(1)} %stack.36, bf16[128,2048]{1,0:T(8,128)(2,1)S(1)} %bitcast.155), kind=kOutput, calls=%fused_computation.82 | convolution fusion | flops 1165013248 | bytes 1106432 | tf_op jit(solution)/shard_map/dot_general | solution.py:269
  26.8 4.8 %shard_map.85 = (bf16[256,2176]{1,0:T(8,128)(2,1)}, bf16[256,2176]{1,0:T(8,128)(2,1)}) custom-call(bf16[16,2176]{1,0:T(8,128)(2,1)} %get-tuple-element.48.picks_ref, f32[1,2176]{1,0:T(1,128)} %get-tuple-element.66.stop_ref, f32[1,2176]{1,0:T(1,128)} %get-tuple-element.65.row_ref), custom_call_target="tpu_custom_call" | custom-call | flops 2000000000 | bytes 2228224 | tf_op jit(solution)/shard_map/pallas_call | solution.py:246
  31.6 4.8 %shard_map.89 = (bf16[256,2176]{1,0:T(8,128)(2,1)}, bf16[256,2176]{1,0:T(8,128)(2,1)}) custom-call(bf16[16,2176]{1,0:T(8,128)(2,1)} %get-tuple-element.47.picks_ref, f32[1,2176]{1,0:T(1,128)} %get-tuple-element.66.stop_ref, f32[1,2176]{1,0:T(1,128)} %get-tuple-element.65.row_ref), custom_call_target="tpu_custom_call" | custom-call | flops 2000000000 | bytes 2228224 | tf_op jit(solution)/shard_map/pallas_call | solution.py:246
  36.4 4.8 %shard_map.91 = (bf16[256,2176]{1,0:T(8,128)(2,1)}, bf16[256,2176]{1,0:T(8,128)(2,1)}) custom-call(bf16[16,2176]{1,0:T(8,128)(2,1)} %get-tuple-element.46.picks_ref, f32[1,2176]{1,0:T(1,128)} %get-tuple-element.66.stop_ref, f32[1,2176]{1,0:T(1,128)} %get-tuple-element.65.row_ref), custom_call_target="tpu_custom_call" | custom-call | flops 2000000000 | bytes 2228224 | tf_op jit(solution)/shard_map/pallas_call | solution.py:246
  41.2 5.4 %shard_map.93 = (bf16[256,2176]{1,0:T(8,128)(2,1)}, bf16[256,2176]{1,0:T(8,128)(2,1)}) custom-call(bf16[16,2176]{1,0:T(8,128)(2,1)} %get-tuple-element.45.picks_ref, f32[1,2176]{1,0:T(1,128)} %get-tuple-element.66.stop_ref, f32[1,2176]{1,0:T(1,128)} %get-tuple-element.65.row_ref), custom_call_target="tpu_custom_call" | custom-call | flops 2000000000 | bytes 2228224 | tf_op jit(solution)/shard_map/pallas_call | solution.py:246
  53.1 3.2 %collective-permute-done.6 = bf16[1,3,64,512]{3,2,1,0:T(8,128)(2,1)S(1)} collective-permute-done((bf16[1,3,64,512]{3,2,1,0:T(8,128)(2,1)S(1)}, bf16[1,3,64,512]{3,2,1,0:T(8,128)(2,1)S(1)}, u32[]{:S(2)}, u32[]{:S(2)}) %collective-permute-start.6) | collective-permute-done | bytes 196640 | tf_op jit(solution)/shard_map/ppermute | solution.py:22
  60.2 6.4 %collective-permute-done.7 = bf16[2,3,64,512]{3,2,1,0:T(8,128)(2,1)S(1)} collective-permute-done((bf16[2,3,64,512]{3,2,1,0:T(8,128)(2,1)S(1)}, bf16[2,3,64,512]{3,2,1,0:T(8,128)(2,1)S(1)}, u32[]{:S(2)}, u32[]{:S(2)}) %collective-permute-start.7) | collective-permute-done | bytes 393248 | tf_op jit(solution)/shard_map/ppermute | solution.py:22
  68.1 4.8 %shard_map.87 = (bf16[256,2176]{1,0:T(8,128)(2,1)}, bf16[256,2176]{1,0:T(8,128)(2,1)}) custom-call(bf16[16,2176]{1,0:T(8,128)(2,1)} %get-tuple-element.58.picks_ref, f32[1,2176]{1,0:T(1,128)} %get-tuple-element.68.stop_ref, f32[1,2176]{1,0:T(1,128)} %get-tuple-element.67.row_ref), custom_call_target="tpu_custom_call" | custom-call | flops 2000000000 | bytes 2228224 | tf_op jit(solution)/shard_map/pallas_call | solution.py:246
  72.9 4.8 %shard_map.90 = (bf16[256,2176]{1,0:T(8,128)(2,1)}, bf16[256,2176]{1,0:T(8,128)(2,1)}) custom-call(bf16[16,2176]{1,0:T(8,128)(2,1)} %get-tuple-element.57.picks_ref, f32[1,2176]{1,0:T(1,128)} %get-tuple-element.68.stop_ref, f32[1,2176]{1,0:T(1,128)} %get-tuple-element.67.row_ref), custom_call_target="tpu_custom_call" | custom-call | flops 2000000000 | bytes 2228224 | tf_op jit(solution)/shard_map/pallas_call | solution.py:246
  77.7 4.8 %shard_map.92 = (bf16[256,2176]{1,0:T(8,128)(2,1)}, bf16[256,2176]{1,0:T(8,128)(2,1)}) custom-call(bf16[16,2176]{1,0:T(8,128)(2,1)} %get-tuple-element.56.picks_ref, f32[1,2176]{1,0:T(1,128)} %get-tuple-element.68.stop_ref, f32[1,2176]{1,0:T(1,128)} %get-tuple-element.67.row_ref), custom_call_target="tpu_custom_call" | custom-call | flops 2000000000 | bytes 2228224 | tf_op jit(solution)/shard_map/pallas_call | solution.py:246
  82.5 4.9 %shard_map.94 = (bf16[256,2176]{1,0:T(8,128)(2,1)}, bf16[256,2176]{1,0:T(8,128)(2,1)}) custom-call(bf16[16,2176]{1,0:T(8,128)(2,1)} %get-tuple-element.55.picks_ref, f32[1,2176]{1,0:T(1,128)} %get-tuple-element.68.stop_ref, f32[1,2176]{1,0:T(1,128)} %get-tuple-element.67.row_ref), custom_call_target="tpu_custom_call" | custom-call | flops 2000000000 | bytes 2228224 | tf_op jit(solution)/shard_map/pallas_call | solution.py:246
  90.0 8.2 %shard_map.86 = bf16[2176,512]{1,0:T(8,128)(2,1)} custom-call(s32[1]{0:T(128)} %bitcast.7.me_ref, s32[2,8]{1,0:T(2,128)} %pad_add_fusion.slots, s32[8]{0:T(128)} %copy-done.11, s32[8]{0:T(128)} %get-tuple-element.74.counts_ref.ct0, bf16[2176,512]{1,0:T(8,128)(2,1)} %fusion.6.x_ref.x0, bf16[2,512,512]{2,1,0:T(8,128)(2,1)} %rel_ref.5, ...), custom_call_target="tpu_custom_call" | custom-call | flops 2147483648 | tf_op jit(solution)/shard_map/pallas_call | solution.py:132
  98.3 2.9 %fusion.74 = bf16[128,2176]{1,0:T(8,128)(2,1)S(1)} fusion(bf16[2176,512]{1,0:T(8,128)(2,1)} %shard_map.86, bf16[128,512]{1,0:T(8,128)(2,1)S(1)} %get-tuple-element.51, bf16[256,2176]{1,0:T(8,128)(2,1)} %get-tuple-element.20, bf16[256,2176]{1,0:T(8,128)(2,1)} %get-tuple-element.19), kind=kOutput, calls=%fused_computation.98 | convolution fusion | flops 286883840 | bytes 4030464 | tf_op jit(solution)/shard_map/dot_general | solution.py:301
  106.4 8.2 %shard_map.88 = bf16[2176,512]{1,0:T(8,128)(2,1)} custom-call(s32[1]{0:T(128)} %bitcast.7.me_ref, s32[2,8]{1,0:T(2,128)} %pad_add_fusion.slots, s32[8]{0:T(128)} %get-tuple-element.72.starts_ref.st1, s32[8]{0:T(128)} %get-tuple-element.71.counts_ref.ct1, bf16[2176,512]{1,0:T(8,128)(2,1)} %copy-done.4, bf16[2,512,512]{2,1,0:T(8,128)(2,1)} %rel_ref.5, ...), custom_call_target="tpu_custom_call" | custom-call | flops 2147483648 | tf_op jit(solution)/shard_map/pallas_call | solution.py:132
  114.6 2.9 %fusion.73 = bf16[128,2176]{1,0:T(8,128)(2,1)S(1)} fusion(bf16[128,512]{1,0:T(8,128)(2,1)S(1)} %fusion.147, bf16[2176,512]{1,0:T(8,128)(2,1)} %shard_map.88, bf16[256,2176]{1,0:T(8,128)(2,1)} %get-tuple-element.22, bf16[256,2176]{1,0:T(8,128)(2,1)} %get-tuple-element.21), kind=kOutput, calls=%fused_computation.97 | convolution fusion | flops 286883840 | bytes 4030464 | tf_op jit(solution)/shard_map/dot_general | solution.py:301
  118.1 3.3 %collective-permute-start.14 = (bf16[128,512]{1,0:T(8,128)(2,1)S(1)}, bf16[128,512]{1,0:T(8,128)(2,1)S(1)}, u32[]{:S(2)}, u32[]{:S(2)}) collective-permute-start(bf16[128,512]{1,0:T(8,128)(2,1)S(1)} %get-tuple-element.91), channel_id=1, source_target_pairs={{0,8},{8,16},{16,24},{24,0},{1,9},{9,17},{17,25},{25,1},{2,10},{10... | collective-permute-start | bytes 393224 | tf_op jit(solution)/shard_map/ppermute | solution.py:314
  122.8 3.9 %collective-permute-start.21 = (bf16[128,512]{1,0:T(8,128)(2,1)S(1)}, bf16[128,512]{1,0:T(8,128)(2,1)S(1)}, u32[]{:S(2)}, u32[]{:S(2)}) collective-permute-start(bf16[128,512]{1,0:T(8,128)(2,1)S(1)} %get-tuple-element.77), channel_id=1, source_target_pairs={{0,8},{8,16},{16,24},{24,0},{1,9},{9,17},{17,25},{25,1},{2,10},{10... | collective-permute-start | bytes 393224 | tf_op jit(solution)/shard_map/ppermute | solution.py:314
  135.6 2.9 %collective-permute-start.16 = (bf16[128,512]{1,0:T(8,128)(2,1)S(1)}, bf16[128,512]{1,0:T(8,128)(2,1)S(1)}, u32[]{:S(2)}, u32[]{:S(2)}) collective-permute-start(bf16[128,512]{1,0:T(8,128)(2,1)S(1)} %get-tuple-element.95), channel_id=1, source_target_pairs={{0,8},{8,16},{16,24},{24,0},{1,9},{9,17},{17,25},{25,1},{2,10},{10... | collective-permute-start | bytes 393224 | tf_op jit(solution)/shard_map/ppermute | solution.py:314
  140.0 3.8 %collective-permute-start.23 = (bf16[128,512]{1,0:T(8,128)(2,1)S(1)}, bf16[128,512]{1,0:T(8,128)(2,1)S(1)}, u32[]{:S(2)}, u32[]{:S(2)}) collective-permute-start(bf16[128,512]{1,0:T(8,128)(2,1)S(1)} %get-tuple-element.81), channel_id=1, source_target_pairs={{0,8},{8,16},{16,24},{24,0},{1,9},{9,17},{17,25},{25,1},{2,10},{10... | collective-permute-start | bytes 393224 | tf_op jit(solution)/shard_map/ppermute | solution.py:314
  157.8 3.2 %collective-permute-start.25 = (bf16[128,512]{1,0:T(8,128)(2,1)S(1)}, bf16[128,512]{1,0:T(8,128)(2,1)S(1)}, u32[]{:S(2)}, u32[]{:S(2)}) collective-permute-start(bf16[128,512]{1,0:T(8,128)(2,1)S(1)} %get-tuple-element.85), channel_id=1, source_target_pairs={{0,8},{8,16},{16,24},{24,0},{1,9},{9,17},{17,25},{25,1},{2,10},{10... | collective-permute-start | bytes 393224 | tf_op jit(solution)/shard_map/ppermute | solution.py:314
  170.8 6.4 %collective-permute-start.28 = (bf16[2176,512]{1,0:T(8,128)(2,1)S(1)}, bf16[2176,512]{1,0:T(8,128)(2,1)S(1)}, u32[]{:S(2)}, u32[]{:S(2)}) collective-permute-start(bf16[2176,512]{1,0:T(8,128)(2,1)S(1)} %fusion.7.g1), channel_id=1, source_target_pairs={{0,4},{4,0},{8,12},{12,8},{16,20},{20,16},{24,28},{28,24},{1,5},{5... | collective-permute-start | bytes 6684680 | tf_op jit(solution)/shard_map/ppermute | solution.py:22
  181.6 2.8 %fusion.201 = (bf16[2176,512]{1,0:T(8,128)(2,1)}, bf16[2176,512]{1,0:T(8,128)(2,1)}) fusion(bf16[2176,512]{1,0:T(8,128)(2,1)S(1)} %collective-permute-done.28, f32[2176,512]{1,0:T(8,128)S(1)} %convolution_add_fusion.4, bf16[128,512]{1,0:T(8,128)(2,1)S(1)} %fusion.159, bf16[128,512]{1,0:T(8,128)(2,1)S(1)} %fusion.152, bf16[128,2176]{1,0:T(8,128)(2,1)S(1)} %fusion.60, ...), kind=kOutput, calls=%fused_computation.336 | convolution fusion | flops 578748416 | bytes 12517376 | tf_op jit(solution)/shard_map/dot_general | solution.py:316
  184.4 7.4 %shard_map.96 = bf16[8,4,2,64,256]{4,3,2,1,0:T(8,128)(2,1)} custom-call(s32[8]{0:T(128)} %get-tuple-element.105.slot_ref, s32[4]{0:T(128)} %and_select_fusion.away_ref, s32[8]{0:T(128)} %copy-done.11, s32[8]{0:T(128)} %get-tuple-element.74.counts_ref.ct0, s32[8]{0:T(128)} %get-tuple-element.72.starts_ref.st1, s32[8]{0:T(128)} %get-tuple-element.71.counts_ref.ct1, ...), custom_call_target="tpu_custom_call" | custom-call | flops 2147483648 | tf_op jit(solution)/shard_map/pallas_call | solution.py:177
  193.4 7.4 %shard_map.97 = bf16[8,4,2,64,256]{4,3,2,1,0:T(8,128)(2,1)} custom-call(s32[8]{0:T(128)} %get-tuple-element.106.slot_ref, s32[4]{0:T(128)} %and_select_fusion.away_ref, s32[8]{0:T(128)} %copy-done.11, s32[8]{0:T(128)} %get-tuple-element.74.counts_ref.ct0, s32[8]{0:T(128)} %get-tuple-element.72.starts_ref.st1, s32[8]{0:T(128)} %get-tuple-element.71.counts_ref.ct1, ...), custom_call_target="tpu_custom_call" | custom-call | flops 2147483648 | tf_op jit(solution)/shard_map/pallas_call | solution.py:177
  205.7 8.7 %shard_map.95 = bf16[2176,512]{1,0:T(8,128)(2,1)} custom-call(s32[1]{0:T(128)} %bitcast.7.me_ref, s32[2,8]{1,0:T(2,128)} %pad_add_fusion.slots, s32[8]{0:T(128)} %copy-done.11, s32[8]{0:T(128)} %get-tuple-element.74.counts_ref.ct0, bf16[2176,512]{1,0:T(8,128)(2,1)} %get-tuple-element.44.x_ref, bf16[2,512,512]{2,1,0:T(8,128)(2,1)} %rel_ref.5, ...), custom_call_target="tpu_custom_call" | custom-call | flops 2147483648 | tf_op jit(solution)/shard_map/pallas_call | solution.py:132
  217.9 6.3 %fusion.75 = bf16[2048,512]{1,0:T(8,128)(2,1)} fusion(bf16[2176,512]{1,0:T(8,128)(2,1)S(1)} %copy-done.8, s32[2048]{0:T(1024)S(1)} %bitcast.160), kind=kOutput, calls=%fused_computation.99 | convolution fusion | flops 4568907776 | bytes 4333568 | tf_op jit(solution)/shard_map/dot_general | solution.py:335
  224.1 5.0 %collective-permute-done.30 = bf16[2,4,2,64,256]{4,3,2,1,0:T(8,128)(2,1)S(1)} collective-permute-done((bf16[2,4,2,64,256]{4,3,2,1,0:T(8,128)(2,1)S(1)}, bf16[2,4,2,64,256]{4,3,2,1,0:T(8,128)(2,1)S(1)}, u32[]{:S(2)}, u32[]{:S(2)}) %collective-permute-start.30) | collective-permute-done | bytes 524320 | tf_op jit(solution)/shard_map/ppermute | solution.py:22
  231.9 5.2 %collective-permute-done.31 = bf16[1,4,2,64,256]{4,3,2,1,0:T(8,128)(2,1)S(1)} collective-permute-done((bf16[1,4,2,64,256]{4,3,2,1,0:T(8,128)(2,1)S(1)}, bf16[1,4,2,64,256]{4,3,2,1,0:T(8,128)(2,1)S(1)}, u32[]{:S(2)}, u32[]{:S(2)}) %collective-permute-start.31) | collective-permute-done | bytes 262176 | tf_op jit(solution)/shard_map/ppermute | solution.py:22
  239.4 3.0 %collective-permute-start.38 = (bf16[2,64,256]{2,1,0:T(8,128)(2,1)S(1)}, bf16[2,64,256]{2,1,0:T(8,128)(2,1)S(1)}, u32[]{:S(2)}, u32[]{:S(2)}) collective-permute-start(bf16[2,64,256]{2,1,0:T(8,128)(2,1)S(1)} %get-tuple-element.62), channel_id=1, source_target_pairs={{1,0},{2,1},{3,2},{0,3},{5,4},{6,5},{7,6},{4,7},{9,8},{10,9},{11,1... | collective-permute-start | bytes 196616 | tf_op jit(solution)/shard_map/ppermute | solution.py:18
  244.4 3.0 %collective-permute-done.33 = bf16[2,64,256]{2,1,0:T(8,128)(2,1)S(1)} collective-permute-done((bf16[2,64,256]{2,1,0:T(8,128)(2,1)S(1)}, bf16[2,64,256]{2,1,0:T(8,128)(2,1)S(1)}, u32[]{:S(2)}, u32[]{:S(2)}) %collective-permute-start.33) | collective-permute-done | bytes 65568 | tf_op jit(solution)/shard_map/ppermute | solution.py:18
  (239 shorter events, 92.4 us)
Async XLA Ops:
  1.7 46.1 %collective-permute-start.1 = (bf16[128,512]{1,0:T(8,128)(2,1)S(1)}, bf16[128,512]{1,0:T(8,128)(2,1)}, u32[]{:S(2)}, u32[]{:S(2)}) collective-permute-start(bf16[128,512]{1,0:T(8,128)(2,1)S(1)} %constant_dynamic-slice_fusion), channel_id=1, source_target_pairs={{2,0},{3,1},{0,2},{1,3},{6,4},{7,5},{4,6},{5,7},{10,8},{11,9},{8,1... | collective-permute-start | bytes 393224 | tf_op jit(solution)/shard_map/ppermute | solution.py:18
  5.8 42.4 %collective-permute-start.2 = (bf16[128,512]{1,0:T(8,128)(2,1)S(1)}, bf16[128,512]{1,0:T(8,128)(2,1)}, u32[]{:S(2)}, u32[]{:S(2)}) collective-permute-start(bf16[128,512]{1,0:T(8,128)(2,1)S(1)} %constant_dynamic-slice_fusion), channel_id=1, source_target_pairs={{3,0},{0,1},{1,2},{2,3},{7,4},{4,5},{5,6},{6,7},{11,8},{8,9},{9,10... | collective-permute-start | bytes 393224 | tf_op jit(solution)/shard_map/ppermute | solution.py:18
  7.4 40.9 %collective-permute-start = (bf16[128,512]{1,0:T(8,128)(2,1)S(1)}, bf16[128,512]{1,0:T(8,128)(2,1)}, u32[]{:S(2)}, u32[]{:S(2)}) collective-permute-start(bf16[128,512]{1,0:T(8,128)(2,1)S(1)} %constant_dynamic-slice_fusion), channel_id=1, source_target_pairs={{1,0},{2,1},{3,2},{0,3},{5,4},{6,5},{7,6},{4,7},{9,8},{10,9},{11,1... | collective-permute-start | bytes 393224 | tf_op jit(solution)/shard_map/ppermute | solution.py:18
  18.2 86.8 %collective-permute-start.13 = (bf16[2176,512]{1,0:T(8,128)(2,1)}, bf16[2176,512]{1,0:T(8,128)(2,1)S(1)}, u32[]{:S(2)}, u32[]{:S(2)}) collective-permute-start(bf16[2176,512]{1,0:T(8,128)(2,1)} %fusion.6.x_ref.x0), channel_id=1, source_target_pairs={{0,4},{4,0},{8,12},{12,8},{16,20},{20,16},{24,28},{28,24},{1,5},{5... | collective-permute-start | bytes 6684680 | tf_op jit(solution)/shard_map/ppermute | solution.py:22
  19.4 27.7 %collective-permute-start.12 = (s32[2,8]{1,0:T(2,128)}, s32[2,8]{1,0:T(2,128)S(1)}, u32[]{:S(2)}, u32[]{:S(2)}) collective-permute-start(s32[2,8]{1,0:T(2,128)} %pad_add_fusion.1), channel_id=1, source_target_pairs={{0,4},{4,0},{8,12},{12,8},{16,20},{20,16},{24,28},{28,24},{1,5},{5... | collective-permute-start | bytes 200 | tf_op jit(solution)/shard_map/ppermute | solution.py:22
  47.2 5.3 %collective-permute-start.11 = (bf16[2,2176]{1,0:T(2,128)(2,1)S(1)}, bf16[2,2176]{1,0:T(2,128)(2,1)S(1)}, u32[]{:S(2)}, u32[]{:S(2)}) collective-permute-start(bf16[2,2176]{1,0:T(2,128)(2,1)S(1)} %get-tuple-element.49), channel_id=1, source_target_pairs={{0,4},{4,0},{8,12},{12,8},{16,20},{20,16},{24,28},{28,24},{1,5},{5... | collective-permute-start | bytes 26120 | tf_op jit(solution)/shard_map/ppermute | solution.py:22
  47.8 11.7 %collective-permute-start.10 = (bf16[4,16,2176]{2,1,0:T(8,128)(2,1)S(1)}, bf16[4,16,2176]{2,1,0:T(8,128)(2,1)S(1)}, u32[]{:S(2)}, u32[]{:S(2)}) collective-permute-start(bf16[4,16,2176]{2,1,0:T(8,128)(2,1)S(1)} %slice.261), channel_id=1, source_target_pairs={{0,4},{4,0},{8,12},{12,8},{16,20},{20,16},{24,28},{28,24},{1,5},{5... | collective-permute-start | bytes 835592 | tf_op jit(solution)/shard_map/ppermute | solution.py:22
  49.4 6.9 %collective-permute-start.6 = (bf16[1,3,64,512]{3,2,1,0:T(8,128)(2,1)S(1)}, bf16[1,3,64,512]{3,2,1,0:T(8,128)(2,1)S(1)}, u32[]{:S(2)}, u32[]{:S(2)}) collective-permute-start(bf16[1,3,64,512]{3,2,1,0:T(8,128)(2,1)S(1)} %get-tuple-element.53), channel_id=1, source_target_pairs={{0,16},{4,20},{8,24},{12,28},{16,0},{20,4},{24,8},{28,12},{1,17},{... | collective-permute-start | bytes 589832 | tf_op jit(solution)/shard_map/ppermute | solution.py:22
  51.0 6.9 %collective-permute-start.3 = (bf16[1,3,64,512]{3,2,1,0:T(8,128)(2,1)S(1)}, bf16[1,3,64,512]{3,2,1,0:T(8,128)(2,1)S(1)}, u32[]{:S(2)}, u32[]{:S(2)}) collective-permute-start(bf16[1,3,64,512]{3,2,1,0:T(8,128)(2,1)S(1)} %get-tuple-element.54), channel_id=1, source_target_pairs={{0,8},{4,12},{8,0},{12,4},{16,24},{20,28},{24,16},{28,20},{1,9},{5... | collective-permute-start | bytes 589832 | tf_op jit(solution)/shard_map/ppermute | solution.py:22
  56.3 10.3 %collective-permute-start.7 = (bf16[2,3,64,512]{3,2,1,0:T(8,128)(2,1)S(1)}, bf16[2,3,64,512]{3,2,1,0:T(8,128)(2,1)S(1)}, u32[]{:S(2)}, u32[]{:S(2)}) collective-permute-start(bf16[2,3,64,512]{3,2,1,0:T(8,128)(2,1)S(1)} %pad_maximum_fusion.7), channel_id=1, source_target_pairs={{0,8},{4,12},{8,0},{12,4},{16,24},{20,28},{24,16},{28,20},{1,9},{5... | collective-permute-start | bytes 1179656 | tf_op jit(solution)/shard_map/ppermute | solution.py:22
  57.9 10.0 %collective-permute-start.4 = (bf16[2,3,64,512]{3,2,1,0:T(8,128)(2,1)S(1)}, bf16[2,3,64,512]{3,2,1,0:T(8,128)(2,1)S(1)}, u32[]{:S(2)}, u32[]{:S(2)}) collective-permute-start(bf16[2,3,64,512]{3,2,1,0:T(8,128)(2,1)S(1)} %pad_maximum_fusion.6), channel_id=1, source_target_pairs={{0,16},{4,20},{8,24},{12,28},{16,0},{20,4},{24,8},{28,12},{1,17},{... | collective-permute-start | bytes 1179656 | tf_op jit(solution)/shard_map/ppermute | solution.py:22
  66.7 20.8 %collective-permute-start.8 = (bf16[4,3,64,512]{3,2,1,0:T(8,128)(2,1)S(1)}, bf16[4,3,64,512]{3,2,1,0:T(8,128)(2,1)S(1)}, u32[]{:S(2)}, u32[]{:S(2)}) collective-permute-start(bf16[4,3,64,512]{3,2,1,0:T(8,128)(2,1)S(1)} %pad_maximum_fusion.3), channel_id=1, source_target_pairs={{0,4},{4,0},{8,12},{12,8},{16,20},{20,16},{24,28},{28,24},{1,5},{5... | collective-permute-start | bytes 2359304 | tf_op jit(solution)/shard_map/ppermute | solution.py:22
  68.0 20.8 %collective-permute-start.5 = (bf16[4,3,64,512]{3,2,1,0:T(8,128)(2,1)S(1)}, bf16[4,3,64,512]{3,2,1,0:T(8,128)(2,1)S(1)}, u32[]{:S(2)}, u32[]{:S(2)}) collective-permute-start(bf16[4,3,64,512]{3,2,1,0:T(8,128)(2,1)S(1)} %pad_maximum_fusion.2), channel_id=1, source_target_pairs={{0,4},{4,0},{8,12},{12,8},{16,20},{20,16},{24,28},{28,24},{1,5},{5... | collective-permute-start | bytes 2359304 | tf_op jit(solution)/shard_map/ppermute | solution.py:22
  118.1 9.5 %collective-permute-start.14 = (bf16[128,512]{1,0:T(8,128)(2,1)S(1)}, bf16[128,512]{1,0:T(8,128)(2,1)S(1)}, u32[]{:S(2)}, u32[]{:S(2)}) collective-permute-start(bf16[128,512]{1,0:T(8,128)(2,1)S(1)} %get-tuple-element.91), channel_id=1, source_target_pairs={{0,8},{8,16},{16,24},{24,0},{1,9},{9,17},{17,25},{25,1},{2,10},{10... | collective-permute-start | bytes 393224 | tf_op jit(solution)/shard_map/ppermute | solution.py:314
  122.8 7.9 %collective-permute-start.21 = (bf16[128,512]{1,0:T(8,128)(2,1)S(1)}, bf16[128,512]{1,0:T(8,128)(2,1)S(1)}, u32[]{:S(2)}, u32[]{:S(2)}) collective-permute-start(bf16[128,512]{1,0:T(8,128)(2,1)S(1)} %get-tuple-element.77), channel_id=1, source_target_pairs={{0,8},{8,16},{16,24},{24,0},{1,9},{9,17},{17,25},{25,1},{2,10},{10... | collective-permute-start | bytes 393224 | tf_op jit(solution)/shard_map/ppermute | solution.py:314
  135.6 8.9 %collective-permute-start.16 = (bf16[128,512]{1,0:T(8,128)(2,1)S(1)}, bf16[128,512]{1,0:T(8,128)(2,1)S(1)}, u32[]{:S(2)}, u32[]{:S(2)}) collective-permute-start(bf16[128,512]{1,0:T(8,128)(2,1)S(1)} %get-tuple-element.95), channel_id=1, source_target_pairs={{0,8},{8,16},{16,24},{24,0},{1,9},{9,17},{17,25},{25,1},{2,10},{10... | collective-permute-start | bytes 393224 | tf_op jit(solution)/shard_map/ppermute | solution.py:314
  140.0 7.9 %collective-permute-start.23 = (bf16[128,512]{1,0:T(8,128)(2,1)S(1)}, bf16[128,512]{1,0:T(8,128)(2,1)S(1)}, u32[]{:S(2)}, u32[]{:S(2)}) collective-permute-start(bf16[128,512]{1,0:T(8,128)(2,1)S(1)} %get-tuple-element.81), channel_id=1, source_target_pairs={{0,8},{8,16},{16,24},{24,0},{1,9},{9,17},{17,25},{25,1},{2,10},{10... | collective-permute-start | bytes 393224 | tf_op jit(solution)/shard_map/ppermute | solution.py:314
  153.7 7.8 %collective-permute-start.18 = (bf16[128,512]{1,0:T(8,128)(2,1)S(1)}, bf16[128,512]{1,0:T(8,128)(2,1)S(1)}, u32[]{:S(2)}, u32[]{:S(2)}) collective-permute-start(bf16[128,512]{1,0:T(8,128)(2,1)S(1)} %get-tuple-element.99), channel_id=1, source_target_pairs={{0,8},{8,16},{16,24},{24,0},{1,9},{9,17},{17,25},{25,1},{2,10},{10... | collective-permute-start | bytes 393224 | tf_op jit(solution)/shard_map/ppermute | solution.py:314
  157.8 7.9 %collective-permute-start.25 = (bf16[128,512]{1,0:T(8,128)(2,1)S(1)}, bf16[128,512]{1,0:T(8,128)(2,1)S(1)}, u32[]{:S(2)}, u32[]{:S(2)}) collective-permute-start(bf16[128,512]{1,0:T(8,128)(2,1)S(1)} %get-tuple-element.85), channel_id=1, source_target_pairs={{0,8},{8,16},{16,24},{24,0},{1,9},{9,17},{17,25},{25,1},{2,10},{10... | collective-permute-start | bytes 393224 | tf_op jit(solution)/shard_map/ppermute | solution.py:314
  170.8 10.8 %collective-permute-start.28 = (bf16[2176,512]{1,0:T(8,128)(2,1)S(1)}, bf16[2176,512]{1,0:T(8,128)(2,1)S(1)}, u32[]{:S(2)}, u32[]{:S(2)}) collective-permute-start(bf16[2176,512]{1,0:T(8,128)(2,1)S(1)} %fusion.7.g1), channel_id=1, source_target_pairs={{0,4},{4,0},{8,12},{12,8},{16,20},{20,16},{24,28},{28,24},{1,5},{5... | collective-permute-start | bytes 6684680 | tf_op jit(solution)/shard_map/ppermute | solution.py:22
  193.2 21.2 %collective-permute-start.29 = (bf16[4,4,2,64,256]{4,3,2,1,0:T(8,128)(2,1)S(1)}, bf16[4,4,2,64,256]{4,3,2,1,0:T(8,128)(2,1)S(1)}, u32[]{:S(2)}, u32[]{:S(2)}) collective-permute-start(bf16[4,4,2,64,256]{4,3,2,1,0:T(8,128)(2,1)S(1)} %slice.342), channel_id=1, source_target_pairs={{0,4},{4,0},{8,12},{12,8},{16,20},{20,16},{24,28},{28,24},{1,5},{5... | collective-permute-start | bytes 3145736 | tf_op jit(solution)/shard_map/ppermute | solution.py:22
  202.2 13.6 %collective-permute-start.35 = (bf16[4,4,2,64,256]{4,3,2,1,0:T(8,128)(2,1)S(1)}, bf16[4,4,2,64,256]{4,3,2,1,0:T(8,128)(2,1)S(1)}, u32[]{:S(2)}, u32[]{:S(2)}) collective-permute-start(bf16[4,4,2,64,256]{4,3,2,1,0:T(8,128)(2,1)S(1)} %slice.352), channel_id=1, source_target_pairs={{0,4},{4,0},{8,12},{12,8},{16,20},{20,16},{24,28},{28,24},{1,5},{5... | collective-permute-start | bytes 3145736 | tf_op jit(solution)/shard_map/ppermute | solution.py:22
  214.9 14.3 %collective-permute-start.30 = (bf16[2,4,2,64,256]{4,3,2,1,0:T(8,128)(2,1)S(1)}, bf16[2,4,2,64,256]{4,3,2,1,0:T(8,128)(2,1)S(1)}, u32[]{:S(2)}, u32[]{:S(2)}) collective-permute-start(bf16[2,4,2,64,256]{4,3,2,1,0:T(8,128)(2,1)S(1)} %slice.344), channel_id=1, source_target_pairs={{0,8},{4,12},{8,0},{12,4},{16,24},{20,28},{24,16},{28,20},{1,9},{5... | collective-permute-start | bytes 1572872 | tf_op jit(solution)/shard_map/ppermute | solution.py:22
  216.4 14.3 %collective-permute-start.36 = (bf16[2,4,2,64,256]{4,3,2,1,0:T(8,128)(2,1)S(1)}, bf16[2,4,2,64,256]{4,3,2,1,0:T(8,128)(2,1)S(1)}, u32[]{:S(2)}, u32[]{:S(2)}) collective-permute-start(bf16[2,4,2,64,256]{4,3,2,1,0:T(8,128)(2,1)S(1)} %slice.354), channel_id=1, source_target_pairs={{0,16},{4,20},{8,24},{12,28},{16,0},{20,4},{24,8},{28,12},{1,17},{... | collective-permute-start | bytes 1572872 | tf_op jit(solution)/shard_map/ppermute | solution.py:22
  229.3 7.8 %collective-permute-start.31 = (bf16[1,4,2,64,256]{4,3,2,1,0:T(8,128)(2,1)S(1)}, bf16[1,4,2,64,256]{4,3,2,1,0:T(8,128)(2,1)S(1)}, u32[]{:S(2)}, u32[]{:S(2)}) collective-permute-start(bf16[1,4,2,64,256]{4,3,2,1,0:T(8,128)(2,1)S(1)} %slice.346), channel_id=1, source_target_pairs={{0,16},{4,20},{8,24},{12,28},{16,0},{20,4},{24,8},{28,12},{1,17},{... | collective-permute-start | bytes 786440 | tf_op jit(solution)/shard_map/ppermute | solution.py:22
  230.9 8.4 %collective-permute-start.37 = (bf16[1,4,2,64,256]{4,3,2,1,0:T(8,128)(2,1)S(1)}, bf16[1,4,2,64,256]{4,3,2,1,0:T(8,128)(2,1)S(1)}, u32[]{:S(2)}, u32[]{:S(2)}) collective-permute-start(bf16[1,4,2,64,256]{4,3,2,1,0:T(8,128)(2,1)S(1)} %slice.356), channel_id=1, source_target_pairs={{0,8},{4,12},{8,0},{12,4},{16,24},{20,28},{24,16},{28,20},{1,9},{5... | collective-permute-start | bytes 786440 | tf_op jit(solution)/shard_map/ppermute | solution.py:22
  237.3 5.2 %collective-permute-start.32 = (bf16[2,64,256]{2,1,0:T(8,128)(2,1)S(1)}, bf16[2,64,256]{2,1,0:T(8,128)(2,1)S(1)}, u32[]{:S(2)}, u32[]{:S(2)}) collective-permute-start(bf16[2,64,256]{2,1,0:T(8,128)(2,1)S(1)} %get-tuple-element.59), channel_id=1, source_target_pairs={{1,0},{2,1},{3,2},{0,3},{5,4},{6,5},{7,6},{4,7},{9,8},{10,9},{11,1... | collective-permute-start | bytes 196616 | tf_op jit(solution)/shard_map/ppermute | solution.py:18
  237.3 10.1 %collective-permute-start.33 = (bf16[2,64,256]{2,1,0:T(8,128)(2,1)S(1)}, bf16[2,64,256]{2,1,0:T(8,128)(2,1)S(1)}, u32[]{:S(2)}, u32[]{:S(2)}) collective-permute-start(bf16[2,64,256]{2,1,0:T(8,128)(2,1)S(1)} %get-tuple-element.61), channel_id=1, source_target_pairs={{2,0},{3,1},{0,2},{1,3},{6,4},{7,5},{4,6},{5,7},{10,8},{11,9},{8,1... | collective-permute-start | bytes 196616 | tf_op jit(solution)/shard_map/ppermute | solution.py:18
  238.5 8.9 %collective-permute-start.34 = (bf16[2,64,256]{2,1,0:T(8,128)(2,1)S(1)}, bf16[2,64,256]{2,1,0:T(8,128)(2,1)S(1)}, u32[]{:S(2)}, u32[]{:S(2)}) collective-permute-start(bf16[2,64,256]{2,1,0:T(8,128)(2,1)S(1)} %get-tuple-element.60), channel_id=1, source_target_pairs={{3,0},{0,1},{1,2},{2,3},{7,4},{4,5},{5,6},{6,7},{11,8},{8,9},{9,10... | collective-permute-start | bytes 196616 | tf_op jit(solution)/shard_map/ppermute | solution.py:18
  239.4 8.0 %collective-permute-start.38 = (bf16[2,64,256]{2,1,0:T(8,128)(2,1)S(1)}, bf16[2,64,256]{2,1,0:T(8,128)(2,1)S(1)}, u32[]{:S(2)}, u32[]{:S(2)}) collective-permute-start(bf16[2,64,256]{2,1,0:T(8,128)(2,1)S(1)} %get-tuple-element.62), channel_id=1, source_target_pairs={{1,0},{2,1},{3,2},{0,3},{5,4},{6,5},{7,6},{4,7},{9,8},{10,9},{11,1... | collective-permute-start | bytes 196616 | tf_op jit(solution)/shard_map/ppermute | solution.py:18
  242.5 7.6 %collective-permute-start.39 = (bf16[2,64,256]{2,1,0:T(8,128)(2,1)S(1)}, bf16[2,64,256]{2,1,0:T(8,128)(2,1)S(1)}, u32[]{:S(2)}, u32[]{:S(2)}) collective-permute-start(bf16[2,64,256]{2,1,0:T(8,128)(2,1)S(1)} %get-tuple-element.64), channel_id=1, source_target_pairs={{2,0},{3,1},{0,2},{1,3},{6,4},{7,5},{4,6},{5,7},{10,8},{11,9},{8,1... | collective-permute-start | bytes 196616 | tf_op jit(solution)/shard_map/ppermute | solution.py:18
  242.5 7.6 %collective-permute-start.40 = (bf16[2,64,256]{2,1,0:T(8,128)(2,1)S(1)}, bf16[2,64,256]{2,1,0:T(8,128)(2,1)S(1)}, u32[]{:S(2)}, u32[]{:S(2)}) collective-permute-start(bf16[2,64,256]{2,1,0:T(8,128)(2,1)S(1)} %get-tuple-element.63), channel_id=1, source_target_pairs={{3,0},{0,1},{1,2},{2,3},{7,4},{4,5},{5,6},{6,7},{11,8},{8,9},{9,10... | collective-permute-start | bytes 196616 | tf_op jit(solution)/shard_map/ppermute | solution.py:18
  (40 other events, 153.6 us)
